TPU v7x, 32 devices: a whole 2x2x4 slice. The times are simulated.
32 devices in a mesh: groups: 2 (over x), mp: 2 (over core), dp: 8 (over z, y).
Axes of the slice: x: 2, y: 2, z: 4, core: 2. Of those that a mesh axis runs over, the one named last changes fastest.
Arguments:
- activations: bfloat16 [4, 32, 4096], P(('groups', 'mp'), 'dp'), parts along dimension 0, may hold values from -6 to 6
- out_grads: bfloat16 [4, 32, 14336], P(('groups', 'mp'), 'dp'), parts along dimension 0, may hold values from -6 to 6
- slot_of: int32 [4, 32], P(('groups', 'mp'), 'dp'), parts along dimension 0, may hold values from 0 to 31, each once within a row
- lengths: int32 [4, 4], P(('groups', 'mp')), parts along dimension 0, may hold values from 1 to 10, 32 in all within a row
- weights: bfloat16 [4, 4096, 14336], P(('groups', 'mp'), 'dp'), parts along dimension 0, may hold values from -6 to 6
Outputs:
- merged: float32 [8192, 14336], P(('groups', 'dp'), 'mp'), parts along dimension 0
There are 2 independent parts, one for each index of `groups`. A program takes and returns all parts, laid end to end along the dimension named above; each array names one. Nothing has to cross between parts.
Inputs may be any that keep to these rules, and one draw needn't show every extreme that they name: `slot_of`: each model's row is a permutation of 0..31. Each model's lengths sum to 32 and the largest is 10.
All inputs are finite; a program needn't handle non-finite values.
Results may differ from a plain program's by a relative error of at most 0.0003.
Values may be sent and summed in bfloat16 or wider, within the bound.
A program may use at most 256 MiB of HBM per device.

v0:
```python
import jax
import jax.numpy as jnp
from jax import lax
from jax.sharding import PartitionSpec as P

EXAMPLES = 4


fisher_eps = 1e-08


def place_rows(all_slots, left_all, right_all):
    count = all_slots.shape[0]
    row_of = jnp.zeros((count,), jnp.int32).at[all_slots].set(jnp.arange(count, dtype=jnp.int32))
    return (left_all[row_of], right_all[row_of])


def fisher_block(left_ord, right_ord, lens, span):
    count = left_ord.shape[0]
    ends = jnp.cumsum(lens)
    starts = ends - lens
    offsets = jnp.arange(span, dtype=jnp.int32)
    total = jnp.zeros((left_ord.shape[1], right_ord.shape[1]), jnp.float32)
    for example in range(EXAMPLES):
        begin = starts[example]
        clamped = jnp.minimum(begin, count - span)
        where_at = clamped + offsets
        keep = (where_at >= begin) & (where_at < begin + lens[example])
        left = lax.dynamic_slice_in_dim(left_ord, clamped, span, 0)
        left = jnp.where(keep[:, None], left, jnp.zeros((), jnp.bfloat16))
        right = lax.dynamic_slice_in_dim(right_ord, clamped, span, 0)
        grad = jnp.dot(left.T, right, preferred_element_type=jnp.float32)
        total = total + grad * grad
    return total


def shards(activations, out_grads, slot_of, lengths, weights):
    acts = activations[0]
    grads = out_grads[0]
    slots = slot_of[0]
    lens = lengths[0]
    w_shard = weights[0]
    span = lax.axis_size("dp") * acts.shape[0] // 3
    x_block = lax.all_to_all(acts, "dp", split_axis=1, concat_axis=0, tiled=True)
    all_grads, all_slots = (
        lax.all_gather(grads, "dp", axis=0, tiled=True),
        lax.all_gather(slots, "dp", axis=0, tiled=True),
    )
    left_ord, right_ord = place_rows(all_slots, x_block, all_grads)
    fisher = fisher_block(left_ord, right_ord, lens, span)
    weighted = fisher * w_shard.astype(jnp.float32)
    num_half, den_half = (
        lax.psum_scatter(weighted, "mp", scatter_dimension=1, tiled=True),
        lax.psum_scatter(fisher, "mp", scatter_dimension=1, tiled=True),
    )
    return num_half / (den_half + fisher_eps)


def solution(mesh):
    in_specs = (
        P(("groups", "mp"), "dp", None),
        P(("groups", "mp"), "dp", None),
        P(("groups", "mp"), "dp"),
        P(("groups", "mp"), None),
        P(("groups", "mp"), "dp", None),
    )
    out_specs = P(("groups", "dp"), "mp")
    return jax.shard_map(shards, mesh=mesh, in_specs=in_specs, out_specs=out_specs, check_vma=False)
```

profile of v0, /device:TPU:0, one launch (start us, length us, event | category | flops | bytes accessed | tf_op | source)
XLA Modules:
  0.0 278.0 jit_solution(9393302235378739491)
XLA Ops:
  6.5 7.3 %all-to-all-start = ((bf16[4,8,512]{2,0,1:T(4,128)(2,1)}), bf16[4,8,512]{2,0,1:T(4,128)(2,1)S(1)}, u32[]{:S(2)}, u32[]{:S(2)}) async-start(bf16[4,8,512]{2,0,1:T(4,128)(2,1)} %bitcast.29), calls=%async_computation | async-start | bytes 65536 | tf_op jit(solution)/shard_map/all_to_all | solution.py:44
  13.8 0.0 reduce-scatter.3.cloned.1.call-start
  13.9 0.8 reduce-window.9
  14.7 0.7 bitcast_subtract_fusion
  15.4 0.7 fusion.34
  18.6 1.5 fusion.33
  20.0 1.2 dynamic-slice
  21.9 0.8 bitcast_dynamic-update-slice_fusion
  22.7 11.8 %all-reduce = s32[32]{0:T(128)S(1)} all-reduce(s32[32]{0:T(128)S(1)} %bitcast_dynamic-update-slice_fusion), channel_id=2, replica_groups=mesh['groups'=2,'mp'=2,'dp'=8] {'dp'}, use_global_device_ids=true, to_apply=%add | all-reduce | flops 32 | bytes 256 | tf_op jit(solution)/shard_map/all_gather | solution.py:47
  34.5 0.7 scatter_custom_fusion
  40.2 0.7 compare_and_fusion
  40.9 0.6 compare_and_fusion.2
  41.5 0.6 compare_and_fusion.3
  42.2 1.1 copy.10
  43.3 38.1 %all-gather.1 = bf16[1,32,14336]{2,0,1:T(2,128)(2,1)S(1)} all-gather(bf16[1,4,14336]{2,0,1:T(2,128)(2,1)S(1)} %copy.10), channel_id=3, replica_groups=mesh['groups'=2,'mp'=2,'dp'=8] {'dp'}, dimensions={1}, use_global_device_ids=true | all-gather | bytes 1032192 | tf_op jit(solution)/shard_map/all_gather | solution.py:46
  81.4 0.5 copy.13
  82.0 1.1 gather_fusion.1
  83.1 0.6 compare_and_fusion.1
  83.7 0.0 all-to-all-done
  83.7 0.6 gather_fusion
  84.3 11.8 %fusion.1 = f32[512,14336]{1,0:T(8,128)} fusion(bf16[32,14336]{1,0:T(8,128)(2,1)S(1)} %gather_fusion.1, s32[]{:T(128)S(6)} %select_n.42, bf16[32,512]{1,0:T(8,128)(2,1)S(1)} %gather_fusion, pred[10]{0:T(512)(128)(4,1)S(1)} %compare_and_fusion.1), kind=kOutput, calls=%fused_computation.8 | convolution fusion | flops 146805760 | bytes 29836800 | tf_op jit(solution)/shard_map/dot_general | solution.py:32
  96.1 11.7 %fusion.3 = f32[512,14336]{1,0:T(8,128)} fusion(bf16[32,14336]{1,0:T(8,128)(2,1)S(1)} %gather_fusion.1, s32[]{:T(128)S(6)} %select_n.40, bf16[32,512]{1,0:T(8,128)(2,1)S(1)} %gather_fusion, pred[10]{0:T(512)(128)(4,1)S(1)} %compare_and_fusion.2), kind=kOutput, calls=%fused_computation.10 | convolution fusion | flops 146805760 | bytes 29836800 | tf_op jit(solution)/shard_map/dot_general | solution.py:32
  107.8 11.7 %fusion.5 = f32[512,14336]{1,0:T(8,128)} fusion(bf16[32,14336]{1,0:T(8,128)(2,1)S(1)} %gather_fusion.1, s32[]{:T(128)S(6)} %select_n.38, bf16[32,512]{1,0:T(8,128)(2,1)S(1)} %gather_fusion, pred[10]{0:T(512)(128)(4,1)S(1)} %compare_and_fusion.3), kind=kOutput, calls=%fused_computation.12 | convolution fusion | flops 146805760 | bytes 29836800 | tf_op jit(solution)/shard_map/dot_general | solution.py:32
  119.5 52.8 %convert_multiply_fusion = (f32[512,14336]{1,0:T(8,128)}, f32[512,14336]{1,0:T(8,128)}) fusion(bf16[1,512,14336]{2,1,0:T(8,128)(2,1)} %param.9, bf16[32,14336]{1,0:T(8,128)(2,1)S(1)} %gather_fusion.1, s32[]{:T(128)S(6)} %select_n.44, bf16[32,512]{1,0:T(8,128)(2,1)S(1)} %gather_fusion, pred[10]{0:T(512)(128)(4,1)S(1)} %compare_and_fusion, ...), kind=kOutput, calls=%fused_computation.3 | convolution fusion | flops 212866048 | bytes 161957376 | tf_op jit(solution)/shard_map/dot_general | solution.py:32
  172.3 0.0 reduce-scatter.3.cloned.1.call-update
  172.3 0.0 reduce-scatter.5.cloned.1.call-start
  172.4 0.7 reduce-scatter.5.cloned.1.call-update
  173.1 38.7 %reduce-scatter.3.cloned.1.call-done = f32[512,7168]{1,0:T(8,128)} async-done(((f32[512,14336]{1,0:T(8,128)}), f32[512,7168]{1,0:T(8,128)}) %reduce-scatter.3.cloned.1.call-update) | async-done | bytes 14680080 | tf_op jit(solution)/shard_map/reduce_scatter | solution.py:53
  211.8 43.7 %reduce-scatter.5.cloned.1.call-done = f32[512,7168]{1,0:T(8,128)} async-done(((f32[512,14336]{1,0:T(8,128)}), f32[512,7168]{1,0:T(8,128)}) %reduce-scatter.5.cloned.1.call-update) | async-done | bytes 14680080 | tf_op jit(solution)/shard_map/reduce_scatter | solution.py:54
  255.4 15.7 %add_divide_fusion = f32[512,7168]{1,0:T(8,128)} fusion(f32[512,7168]{1,0:T(8,128)} %reduce-scatter.3.cloned.1.call-done, f32[512,7168]{1,0:T(8,128)} %reduce-scatter.5.cloned.1.call-done), kind=kLoop, calls=%fused_computation.5 | loop fusion | flops 7340032 | bytes 44040192 | tf_op jit(solution)/shard_map/div | solution.py:56
  (6 shorter events, 0.0 us)
Async XLA Ops:
  6.5 77.1 %all-to-all-start = ((bf16[4,8,512]{2,0,1:T(4,128)(2,1)}), bf16[4,8,512]{2,0,1:T(4,128)(2,1)S(1)}, u32[]{:S(2)}, u32[]{:S(2)}) async-start(bf16[4,8,512]{2,0,1:T(4,128)(2,1)} %bitcast.29), calls=%async_computation | async-start | bytes 65536 | tf_op jit(solution)/shard_map/all_to_all | solution.py:44
  13.8 197.9 %reduce-scatter.3.cloned.1.call-start = ((), (), s32[]{:S(2)}) async-start(), calls=%async_computation.3 | async-start | bytes 44040192 | tf_op jit(solution)/shard_map/reduce_scatter | solution.py:53
  172.3 83.1 %reduce-scatter.5.cloned.1.call-start = ((), (), s32[]{:S(2)}) async-start(), calls=%async_computation.4 | async-start | bytes 44040192 | tf_op jit(solution)/shard_map/reduce_scatter | solution.py:54
Sparse Core Ops, SparseCore 0:
  172.4 39.2 reduce-scatter.2
  214.1 41.3 reduce-scatter.4
where the time goes:
time: 278 us
  matrix products  88 us (32%)
  waiting for transfers between devices  83.1 us (30%)
  blocking collectives  49.9 us (18%)
  between operations  21.7 us (8%)
  other arithmetic  19.7 us (7%)
  local copies, waits for them, and re-layouts  8.19 us (3%)
  starting transfers between devices  7.36 us (3%)
    dot_general x4, matrix products, fisher_block(): grad = jnp.dot(left.T, right, preferred_element_type=jnp.float32)  88 us
    reduce_scatter x1, waiting for transfers between devices, shards(): lax.psum_scatter(fisher, 'mp', scatter_dimension=1, tiled=True)  43.7 us
    reduce_scatter x1, waiting for transfers between devices, shards(): lax.psum_scatter(weighted, 'mp', scatter_dimension=1, tiled=True)  38.7 us
    all_gather x1, blocking collectives, shards(): lax.all_gather(grads, 'dp', axis=0, tiled=True)  38.1 us
    div x1, other arithmetic, shards(): return num_half / (den_half + fisher_eps)  15.7 us
    all_gather x1, blocking collectives, shards(): lax.all_gather(slots, 'dp', axis=0, tiled=True)  11.8 us
    all_to_all x1, starting transfers between devices, shards(): lax.all_to_all(acts, 'dp', split_axis=1, concat_axis=0, tiled=True)  7.28 us
  transfers between devices with their start and end apart: 3, of which 2 were waited for; matrix products, arithmetic and copies ran while one was open for 4% of the time, Pallas kernels for 0%

commit v1 on v0

--- a/solution.py
+++ b/solution.py
@@ -1,10 +1,20 @@
+import functools
+
 import jax
 import jax.numpy as jnp
 from jax import lax
+from jax.experimental import pallas as pl
+from jax.experimental.pallas import tpu as pltpu
 from jax.sharding import PartitionSpec as P
 
 EXAMPLES = 4
-
+MODELS = 2
+LANES = 128
+DEPTH = 256
+QUARTERS = 4
+WIDE = 256
+STACK = MODELS * EXAMPLES
+SUB = 64
 
 fisher_eps = 1e-08
 
@@ -34,7 +44,7 @@
     return total
 
 
-def shards(activations, out_grads, slot_of, lengths, weights):
+def shards_general(activations, out_grads, slot_of, lengths, weights):
     acts = activations[0]
     grads = out_grads[0]
     slots = slot_of[0]
@@ -56,6 +66,161 @@
     return num_half / (den_half + fisher_eps)
 
 
+def merge_kernel(sources, groups, x_ref, g_ref, w_ref, out_ref, x_all, g_all, lhs, w_own, w_mate, out_buf,
+                 x_recv, g_recv, w_recv, own_sem, x_send, g_send, w_send, out_sem):
+    mp, dp = lax.axis_index("mp"), lax.axis_index("dp")
+    mate = 1 - mp
+    mine = mp * sources + dp
+    rows, cols = out_ref.shape
+    chunks = g_ref.shape[1]
+    step = QUARTERS * WIDE
+
+    def w_copy(c):
+        return pltpu.make_async_remote_copy(
+            src_ref=w_ref.at[:, pl.ds(pl.multiple_of(mate * cols + c * step, LANES), step)],
+            dst_ref=w_mate.at[:, pl.ds(c * step, step)],
+            send_sem=w_send.at[c],
+            recv_sem=w_recv.at[c],
+            device_id={"mp": mate},
+            device_id_type=pl.DeviceIdType.MESH,
+        )
+
+    def own_copy(c):
+        return pltpu.make_async_copy(
+            w_ref.at[:, pl.ds(pl.multiple_of(mp * cols + c * step, LANES), step)],
+            w_own.at[:, pl.ds(c * step, step)],
+            own_sem.at[c],
+        )
+
+    def out_copy(c):
+        return pltpu.make_async_copy(
+            out_buf.at[c % 2], out_ref.at[:, pl.ds(c * step, step)], out_sem.at[c % 2])
+
+    partners = [(i, k) for k in range(sources) for i in range(MODELS) if (i, k) != (0, 0)]
+    places = [(lax.rem(mp + i, MODELS), lax.rem(dp + k, sources)) for i, k in partners]
+
+    barrier = pltpu.get_barrier_semaphore()
+    for to_mp, to_dp in places:
+        pl.semaphore_signal(barrier, inc=1, device_id={"mp": to_mp, "dp": to_dp},
+                            device_id_type=pl.DeviceIdType.MESH)
+    pltpu.make_async_copy(x_ref.at[dp], x_all.at[mine], x_recv).start()
+    for n, (lo, hi) in enumerate(groups):
+        pltpu.make_async_copy(g_ref.at[mp, pl.ds(lo, hi - lo)], g_all.at[pl.ds(lo, hi - lo), mine],
+                              g_recv.at[n]).start()
+    for c in range(chunks):
+        own_copy(c).start()
+    pl.semaphore_wait(barrier, len(places))
+
+    for to_mp, to_dp in places:
+        pltpu.make_async_remote_copy(
+            src_ref=x_ref.at[to_dp], dst_ref=x_all.at[mine], send_sem=x_send, recv_sem=x_recv,
+            device_id={"mp": to_mp, "dp": to_dp}, device_id_type=pl.DeviceIdType.MESH).start()
+    w_copy(0).start()
+    for n, (lo, hi) in enumerate(groups):
+        for to_mp, to_dp in places:
+            pltpu.make_async_remote_copy(
+                src_ref=g_ref.at[to_mp, pl.ds(lo, hi - lo)], dst_ref=g_all.at[pl.ds(lo, hi - lo), mine],
+                send_sem=g_send.at[n], recv_sem=g_recv.at[n],
+                device_id={"mp": to_mp, "dp": to_dp}, device_id_type=pl.DeviceIdType.MESH).start()
+        if n == 0:
+            for c in range(1, chunks):
+                w_copy(c).start()
+
+    pltpu.make_async_copy(x_all, x_all, x_recv).wait()
+    turned = x_all[...].reshape(DEPTH, -1).astype(jnp.float32).T
+    code = turned[rows:rows + 1, :]
+    left = turned[:rows, :].astype(jnp.bfloat16)
+    for q in range(QUARTERS):
+        for v in range(STACK):
+            which = lax.rem(mp + v // EXAMPLES, MODELS) * EXAMPLES + v % EXAMPLES
+            keep = code == (which * QUARTERS + q).astype(jnp.float32)
+            part = left * keep.astype(jnp.float32).astype(jnp.bfloat16)
+            for t in range(rows // SUB):
+                lhs[q, t, v * SUB:(v + 1) * SUB, :] = part[t * SUB:(t + 1) * SUB, :]
+
+    starts = {lo: n for n, (lo, hi) in enumerate(groups)}
+    for c in range(chunks):
+        if c in starts:
+            lo, hi = groups[starts[c]]
+            whole = g_all.at[pl.ds(lo, hi - lo)]
+            pltpu.make_async_copy(whole, whole, g_recv.at[starts[c]]).wait()
+        own_copy(c).wait()
+        w_copy(c).wait_recv()
+        if c >= 2:
+            out_copy(c - 2).wait()
+
+        @pl.loop(0, rows // SUB)
+        def _(t):
+            at = pl.multiple_of(t * SUB, SUB)
+            for q in range(QUARTERS):
+                right = g_all[c].reshape(DEPTH, WIDE)
+                grads = jnp.dot(lhs[q, t], right, preferred_element_type=jnp.float32)
+                square = grads * grads
+                own, other = [
+                    sum(square[(h * EXAMPLES + e) * SUB:(h * EXAMPLES + e + 1) * SUB] for e in range(EXAMPLES))
+                    for h in range(MODELS)
+                ]
+                here = pl.ds(c * step + q * WIDE, WIDE)
+                top = (own * w_own[pl.ds(at, SUB), here].astype(jnp.float32)
+                       + other * w_mate[pl.ds(at, SUB), here].astype(jnp.float32))
+                out_buf[c % 2, pl.ds(at, SUB), q * WIDE:(q + 1) * WIDE] = top / (own + other + fisher_eps)
+
+        out_copy(c).start()
+
+    for c in range(max(0, chunks - 2), chunks):
+        out_copy(c).wait()
+    for c in range(chunks):
+        w_copy(c).wait_send()
+    sent = x_all.at[pl.ds(0, len(places))]
+    pltpu.make_async_copy(sent, sent, x_send).wait()
+    for n, (lo, hi) in enumerate(groups):
+        sent = g_all.at[pl.ds(lo, hi - lo), pl.ds(0, len(places))]
+        pltpu.make_async_copy(sent, sent, g_send.at[n]).wait()
+
+
+def shards_kernel(activations, out_grads, slot_of, lengths, weights):
+    acts, grads, slots, lens, w_shard = activations[0], out_grads[0], slot_of[0], lengths[0], weights[0]
+    sources = lax.axis_size("dp")
+    tokens, width = acts.shape
+    rows = width // sources
+    cols = grads.shape[1] // MODELS
+    chunks = cols // (QUARTERS * WIDE)
+    packed = QUARTERS * tokens
+    example = jnp.sum((slots[:, None] >= jnp.cumsum(lens)[None, :]).astype(jnp.int32), axis=1)
+    code = (lax.axis_index("mp") * EXAMPLES + example)[None, :] * QUARTERS + jnp.arange(QUARTERS)[:, None]
+    x_part = acts.reshape(tokens, sources, rows).transpose(1, 0, 2)
+    x_part = jnp.broadcast_to(x_part[:, None], (sources, QUARTERS, tokens, rows)).reshape(sources, packed, rows)
+    code = jnp.broadcast_to(code.reshape(1, packed, 1), (sources, packed, LANES)).astype(jnp.bfloat16)
+    x_pack = jnp.concatenate([x_part, code], axis=2)
+    g_pack = grads.reshape(tokens, MODELS, chunks, QUARTERS, WIDE).transpose(1, 2, 3, 0, 4)
+    g_pack = g_pack.reshape(MODELS, chunks, packed, WIDE)
+    groups = ((0, 1), (1, 3), (3, chunks))
+    everyone = MODELS * sources
+    step = QUARTERS * WIDE
+    dma = pltpu.SemaphoreType.DMA
+    return pl.pallas_call(
+        functools.partial(merge_kernel, sources, groups),
+        out_shape=jax.ShapeDtypeStruct((rows, cols), jnp.float32),
+        in_specs=[pl.BlockSpec(memory_space=pl.ANY)] * 3,
+        out_specs=pl.BlockSpec(memory_space=pl.ANY),
+        scratch_shapes=[
+            pltpu.VMEM((everyone, packed, rows + LANES), jnp.bfloat16),
+            pltpu.VMEM((chunks, everyone, packed, WIDE), jnp.bfloat16),
+            pltpu.VMEM((QUARTERS, rows // SUB, STACK * SUB, DEPTH), jnp.bfloat16),
+            pltpu.VMEM((rows, cols), jnp.bfloat16),
+            pltpu.VMEM((rows, cols), jnp.bfloat16),
+            pltpu.VMEM((2, rows, step), jnp.float32),
+            dma, dma((len(groups),)), dma((chunks,)), dma((chunks,)),
+            dma, dma((len(groups),)), dma((chunks,)), dma((2,)),
+        ],
+        compiler_params=pltpu.CompilerParams(
+            collective_id=0, has_side_effects=True, vmem_limit_bytes=56 * 1024 * 1024),
+        cost_estimate=pl.CostEstimate(
+            flops=2 * STACK * rows * cols * DEPTH, bytes_accessed=12 * rows * cols, transcendentals=0),
+        name="merge",
+    )(x_pack, g_pack, w_shard)
+
+
 def solution(mesh):
     in_specs = (
         P(("groups", "mp"), "dp", None),
@@ -65,4 +230,15 @@
         P(("groups", "mp"), "dp", None),
     )
     out_specs = P(("groups", "dp"), "mp")
-    return jax.shard_map(shards, mesh=mesh, in_specs=in_specs, out_specs=out_specs, check_vma=False)
+
+    def merge(activations, out_grads, slot_of, lengths, weights):
+        tokens = activations.shape[1]
+        rows = activations.shape[2] // mesh.shape["dp"]
+        cols = out_grads.shape[2] // MODELS
+        fits = (MODELS * QUARTERS * tokens == DEPTH and (QUARTERS * tokens // mesh.shape["dp"]) % 16 == 0
+                and rows % SUB == 0 and cols % (QUARTERS * WIDE) == 0 and cols // (QUARTERS * WIDE) > 3)
+        body = shards_kernel if fits else shards_general
+        return jax.shard_map(body, mesh=mesh, in_specs=in_specs, out_specs=out_specs, check_vma=False)(
+            activations, out_grads, slot_of, lengths, weights)
+
+    return merge

time: 278 us -> 69.7 us (0.25)
  matrix products: 88 us -> 0 us
  waiting for transfers between devices: 83.1 us -> 0 us
  Pallas kernels: 0 us -> 51.1 us
  blocking collectives: 49.9 us -> 0 us
  between operations: 21.7 us -> 0.03 us
  other arithmetic: 19.7 us -> 2.36 us
  starting transfers between devices: 7.36 us -> 0 us
  local copies, waits for them, and re-layouts: 8.19 us -> 15 us
    dot_general x4 -> x0, matrix products: 88 us -> none  [fisher_block(): grad = jnp.dot(left.T, right, preferred_element_type=jnp.float32)]
    reduce_scatter x2 -> x0, waiting for transfers between devices: 82.4 us -> none  [the longest x1 43.7 us: shards(): lax.psum_scatter(fisher, 'mp', scatter_dimension=1, tiled=True)]
    pallas_call x0 -> x1, Pallas kernels: none -> 51.1 us  [shards_kernel(): pl.pallas_call(functools.partial(merge_kernel, sources, groups), out_shap...]
    all_gather x2 -> x0, blocking collectives: 49.9 us -> none  [the longest x1 38.1 us: shards(): lax.all_gather(grads, 'dp', axis=0, tiled=True)]
    div x1 -> x0, other arithmetic: 15.7 us -> none  [shards(): return num_half / (den_half + fisher_eps)]
    unnamed x4 -> x2, local copies, waits for them, and re-layouts: 3.6 us -> 13.2 us
    all_to_all x1 -> x0, starting transfers between devices: 7.28 us -> none  [shards(): lax.all_to_all(acts, 'dp', split_axis=1, concat_axis=0, tiled=True)]
  transfers between devices with their start and end apart: 3 -> 0, of which waited for: 2 -> 0; matrix products, arithmetic and copies ran while one was open for 4% -> 0% of each run, Pallas kernels for 0% -> 0%
where the time goes in v1:
time: 69.7 us; the launch traced here: 68.5 us
  Pallas kernels  51.1 us (73%)
  local copies, waits for them, and re-layouts  15 us (22%)
  other arithmetic  2.36 us (3%)
    pallas_call x1, Pallas kernels, shards_kernel(): pl.pallas_call(functools.partial(merge_kernel, sources, groups), out_shap...  51.1 us
    unnamed x2, local copies, waits for them, and re-layouts  13.2 us
    reshape x1, local copies, waits for them, and re-layouts, shards_kernel(): g_pack = g_pack.reshape(MODELS, chunks, packed, WIDE)  1.56 us

profile of v1, /device:TPU:0, one launch (start us, length us, event | category | flops | bytes accessed | tf_op | source)
XLA Modules:
  0.0 68.5 jit_solution(475728889217369210)
XLA Ops:
  0.0 0.8 %reduce-window.8 = s32[4,1]{0,1:T(1,128)S(1)} reduce-window(s32[4,1]{0,1:T(1,128)} %bitcast.19, s32[]{:T(128)} %constant.13.clone.1), window={size=4x1 pad=3_0x0_0}, to_apply=%region_0.0 | reduce-window | flops 12 | bytes 36 | tf_op jit(solution)/shard_map/reduce-window.3 | solution.py:241
  0.8 0.8 %convert_reduce_fusion = s32[4]{0:T(128)S(1)} fusion(s32[4]{0:T(128)S(1)} %bitcast.21, s32[4]{0:T(128)} %bitcast.20), kind=kLoop, calls=%fused_computation.3 | loop fusion | flops 44 | bytes 48 | tf_op jit(solution)/shard_map/reduce_sum | solution.py:189
  1.7 0.1 convert_element_type.12
  1.8 0.1 broadcast_in_dim.5
  1.8 0.8 %copy.12 = bf16[1,4,8,512]{3,2,1,0:T(8,128)(2,1)S(1)} copy(bf16[1,4,8,512]{3,1,2,0:T(4,128)(2,1)} %bitcast.17) | data formatting | bytes 65536
  2.7 0.7 pad_maximum_fusion.x_ref
  3.4 1.6 %reshape.56.g_ref = bf16[2,7,16,256]{3,2,1,0:T(8,128)(2,1)} reshape(bf16[2,7,4,4,256]{4,3,2,1,0:T(4,128)(2,1)} %bitcast.16) | data formatting | bytes 229376 | tf_op jit(solution)/shard_map/reshape | solution.py:196
  5.0 51.1 %merge.1 = f32[512,7168]{1,0:T(8,128)} custom-call(bf16[8,16,640]{2,1,0:T(8,128)(2,1)} %pad_maximum_fusion.x_ref, bf16[2,7,16,256]{3,2,1,0:T(8,128)(2,1)} %reshape.56.g_ref, bf16[512,14336]{1,0:T(8,128)(2,1)} %bitcast.18), custom_call_target="tpu_custom_call" | custom-call | flops 15032385536 | bytes 44040192 | tf_op jit(solution)/shard_map/merge/pallas_call | solution.py:201
  56.1 12.4 %copy.14 = f32[512,7168]{1,0:T(8,128)} copy(f32[512,7168]{1,0:T(8,128)} %merge.1) | data formatting | bytes 29360128
  (5 shorter events, 0.1 us)

commit v2 on v0

--- a/solution.py
+++ b/solution.py
@@ -1,10 +1,21 @@
+import functools
+
 import jax
 import jax.numpy as jnp
 from jax import lax
+from jax.experimental import pallas as pl
+from jax.experimental.pallas import tpu as pltpu
 from jax.sharding import PartitionSpec as P
 
 EXAMPLES = 4
-
+MODELS = 2
+LANES = 128
+DEPTH = 256
+QUARTERS = 4
+WIDE = 256
+STACK = MODELS * EXAMPLES
+SUB = 256
+LINES = 2
 
 fisher_eps = 1e-08
 
@@ -34,7 +45,7 @@
     return total
 
 
-def shards(activations, out_grads, slot_of, lengths, weights):
+def shards_general(activations, out_grads, slot_of, lengths, weights):
     acts = activations[0]
     grads = out_grads[0]
     slots = slot_of[0]
@@ -56,6 +67,176 @@
     return num_half / (den_half + fisher_eps)
 
 
+def merge_kernel(sources, x_ref, g_ref, w_ref, out_ref, x_all, g_all, lhs, w_own, w_mate,
+                 x_recv, line_recv, relay_recv, w_recv, own_sem, x_send, line_send, relay_send, w_send):
+    mp, dp = lax.axis_index("mp"), lax.axis_index("dp")
+    mate = 1 - mp
+    line, spot = lax.rem(dp, LINES), lax.div(dp, LINES)
+    length = sources // LINES
+    rows, cols = out_ref.shape
+    chunks = g_ref.shape[1]
+    step = QUARTERS * WIDE
+
+    def send(src, dst, send_sem, recv_sem, to_mp, to_dp):
+        return pltpu.make_async_remote_copy(
+            src_ref=src, dst_ref=dst, send_sem=send_sem, recv_sem=recv_sem,
+            device_id={"mp": to_mp, "dp": to_dp}, device_id_type=pl.DeviceIdType.MESH)
+
+    def w_copy(c):
+        return send(w_ref.at[:, pl.ds(pl.multiple_of(mate * cols + c * step, LANES), step)],
+                    w_mate.at[:, pl.ds(pl.multiple_of(c * step, LANES), step)],
+                    w_send.at[c], w_recv.at[c], mate, dp)
+
+    def own_copy(c):
+        return pltpu.make_async_copy(
+            w_ref.at[:, pl.ds(pl.multiple_of(mp * cols + c * step, LANES), step)],
+            w_own.at[:, pl.ds(pl.multiple_of(c * step, LANES), step)],
+            own_sem.at[c])
+
+    def line_copy(c, to_mp, to_dp):
+        return send(g_ref.at[to_mp, c], g_all.at[c, line, spot, mp], line_send.at[c], line_recv.at[c], to_mp, to_dp)
+
+    def relay_copy(c):
+        return send(g_all.at[c, line], g_all.at[c, line], relay_send.at[c], relay_recv.at[c],
+                    mp, spot * LINES + 1 - line)
+
+    def relay(c):
+        whole = g_all.at[c, line]
+        pltpu.make_async_copy(whole, whole, line_recv.at[c]).wait()
+        relay_copy(c).start()
+
+    offsets = [(i, k) for k in range(sources) for i in range(MODELS) if (i, k) != (0, 0)]
+    places = [(lax.rem(mp + i, MODELS), lax.rem(dp + k, sources)) for i, k in offsets]
+    in_line = [(lax.rem(mp + i, MODELS), lax.rem(dp + k * LINES, sources))
+               for k in range(length) for i in range(MODELS) if (i, k) != (0, 0)]
+
+    barrier = pltpu.get_barrier_semaphore()
+    for to_mp, to_dp in places:
+        pl.semaphore_signal(barrier, inc=1, device_id={"mp": to_mp, "dp": to_dp},
+                            device_id_type=pl.DeviceIdType.MESH)
+    pltpu.make_async_copy(x_ref.at[dp], x_all.at[line, spot, mp], x_recv).start()
+
+    @pl.loop(0, chunks)
+    def _(c):
+        pltpu.make_async_copy(g_ref.at[mp, c], g_all.at[c, line, spot, mp], line_recv.at[c]).start()
+        own_copy(c).start()
+
+    pl.semaphore_wait(barrier, len(places))
+    for to_mp, to_dp in in_line:
+        line_copy(0, to_mp, to_dp).start()
+    for to_mp, to_dp in places:
+        send(x_ref.at[to_dp], x_all.at[line, spot, mp], x_send, x_recv, to_mp, to_dp).start()
+    w_copy(0).start()
+
+    @pl.loop(1, chunks)
+    def _(c):
+        for to_mp, to_dp in in_line:
+            line_copy(c, to_mp, to_dp).start()
+        w_copy(c).start()
+
+    relay(0)
+    relay(1)
+
+    pltpu.make_async_copy(x_all, x_all, x_recv).wait()
+    arrived = x_all[...].reshape(DEPTH, 2 * LANES).astype(jnp.float32).T
+    code = arrived[LANES:LANES + 1, :]
+    arrived = arrived[:LANES, :].astype(jnp.bfloat16)
+    tokens = DEPTH // (MODELS * sources * QUARTERS)
+    packed = QUARTERS * tokens
+    source = lax.broadcasted_iota(jnp.int32, (DEPTH, DEPTH), 0)
+    target = lax.broadcasted_iota(jnp.int32, (DEPTH, DEPTH), 1)
+    same = (source // packed == target // packed) & (source % tokens == target % tokens)
+    for p in range(rows // LANES):
+        spread = (same & (source % packed // tokens == p)).astype(jnp.float32).astype(jnp.bfloat16)
+        left = jnp.dot(arrived, spread, preferred_element_type=jnp.float32).astype(jnp.bfloat16)
+        t, base = p * LANES // SUB, p * LANES % SUB
+        for q in range(QUARTERS):
+            for v in range(STACK):
+                which = lax.rem(mp + v // EXAMPLES, MODELS) * EXAMPLES + v % EXAMPLES
+                keep = code == (which * QUARTERS + q).astype(jnp.float32)
+                lhs[q, t, v * SUB + base:v * SUB + base + LANES, :] = left * keep.astype(jnp.float32).astype(jnp.bfloat16)
+
+    @pl.loop(0, chunks)
+    def _(c):
+        @pl.when(c + 2 < chunks)
+        def _():
+            relay(c + 2)
+
+        other_line = g_all.at[c, 1 - line]
+        pltpu.make_async_copy(other_line, other_line, relay_recv.at[c]).wait()
+        own_copy(c).wait()
+        w_copy(c).wait_recv()
+
+        @pl.loop(0, rows // SUB)
+        def _(t):
+            at = pl.ds(pl.multiple_of(t * SUB, SUB), SUB)
+            for q in range(QUARTERS):
+                right = g_all[c].reshape(DEPTH, WIDE)
+                fishers = []
+                for h in range(MODELS):
+                    fisher = jnp.zeros((SUB, WIDE), jnp.float32)
+                    for e in range(EXAMPLES):
+                        v = h * EXAMPLES + e
+                        grad = jnp.dot(lhs[q, t, v * SUB:(v + 1) * SUB, :], right, preferred_element_type=jnp.float32)
+                        fisher = fisher + grad * grad
+                    fishers.append(fisher)
+                own, other = fishers
+                here = pl.ds(pl.multiple_of(c * step + q * WIDE, LANES), WIDE)
+                top = own * w_own[at, here].astype(jnp.float32) + other * w_mate[at, here].astype(jnp.float32)
+                out_ref[at, here] = top / (own + other + fisher_eps)
+
+    blocks = lambda count: lhs.at[0, 0, pl.ds(0, count * packed)]
+    pltpu.make_async_copy(blocks(len(places)), blocks(len(places)), x_send).wait()
+
+    @pl.loop(0, chunks)
+    def _(c):
+        pltpu.make_async_copy(blocks(len(in_line)), blocks(len(in_line)), line_send.at[c]).wait()
+        relay_copy(c).wait_send()
+        w_copy(c).wait_send()
+
+
+def shards_kernel(activations, out_grads, slot_of, lengths, weights):
+    acts, grads, slots, lens, w_shard = activations[0], out_grads[0], slot_of[0], lengths[0], weights[0]
+    sources = lax.axis_size("dp")
+    tokens, width = acts.shape
+    rows = width // sources
+    cols = grads.shape[1] // MODELS
+    chunks = cols // (QUARTERS * WIDE)
+    packed = QUARTERS * tokens
+    example, end = jnp.zeros((tokens,), jnp.int32), 0
+    for e in range(EXAMPLES - 1):
+        end = end + lens[e]
+        example = example + (slots >= end).astype(jnp.int32)
+    code = (lax.axis_index("mp") * EXAMPLES + example)[None, :] * QUARTERS + jnp.arange(QUARTERS)[:, None]
+    x_part = acts.reshape(tokens, sources, rows // LANES, LANES).transpose(1, 2, 0, 3).reshape(sources, packed, LANES)
+    code = jnp.broadcast_to(code.reshape(1, packed, 1), (sources, packed, LANES)).astype(jnp.bfloat16)
+    x_pack = jnp.concatenate([x_part, code], axis=2)
+    g_pack = grads.reshape(tokens, MODELS, chunks, QUARTERS, WIDE).transpose(1, 2, 3, 0, 4)
+    g_pack = g_pack.reshape(MODELS, chunks, packed, WIDE)
+    length = sources // LINES
+    dma = pltpu.SemaphoreType.DMA
+    return pl.pallas_call(
+        functools.partial(merge_kernel, sources),
+        out_shape=pltpu.VMEM((rows, cols), jnp.float32),
+        in_specs=[pl.BlockSpec(memory_space=pl.ANY)] * 3,
+        out_specs=pl.BlockSpec(memory_space=pltpu.VMEM),
+        scratch_shapes=[
+            pltpu.VMEM((LINES, length, MODELS, packed, 2 * LANES), jnp.bfloat16),
+            pltpu.VMEM((chunks, LINES, length, MODELS, packed, WIDE), jnp.bfloat16),
+            pltpu.VMEM((QUARTERS, rows // SUB, STACK * SUB, DEPTH), jnp.bfloat16),
+            pltpu.VMEM((rows, cols), jnp.bfloat16),
+            pltpu.VMEM((rows, cols), jnp.bfloat16),
+            dma, dma((chunks,)), dma((chunks,)), dma((chunks,)), dma((chunks,)),
+            dma, dma((chunks,)), dma((chunks,)), dma((chunks,)),
+        ],
+        compiler_params=pltpu.CompilerParams(
+            collective_id=0, has_side_effects=True, vmem_limit_bytes=40 * 1024 * 1024),
+        cost_estimate=pl.CostEstimate(
+            flops=2 * STACK * rows * cols * DEPTH, bytes_accessed=12 * rows * cols, transcendentals=0),
+        name="merge",
+    )(x_pack, g_pack, w_shard)
+
+
 def solution(mesh):
     in_specs = (
         P(("groups", "mp"), "dp", None),
@@ -65,4 +246,15 @@
         P(("groups", "mp"), "dp", None),
     )
     out_specs = P(("groups", "dp"), "mp")
-    return jax.shard_map(shards, mesh=mesh, in_specs=in_specs, out_specs=out_specs, check_vma=False)
+
+    def merge(activations, out_grads, slot_of, lengths, weights):
+        tokens = activations.shape[1]
+        rows = activations.shape[2] // mesh.shape["dp"]
+        cols = out_grads.shape[2] // MODELS
+        fits = (MODELS * QUARTERS * tokens == DEPTH and (QUARTERS * tokens // mesh.shape["dp"]) % 16 == 0
+                and rows % SUB == 0 and rows == QUARTERS * LANES and cols % (QUARTERS * WIDE) == 0 and cols // (QUARTERS * WIDE) > 3)
+        body = shards_kernel if fits else shards_general
+        return jax.shard_map(body, mesh=mesh, in_specs=in_specs, out_specs=out_specs, check_vma=False)(
+            activations, out_grads, slot_of, lengths, weights)
+
+    return merge

time: 278 us -> 50.3 us (0.18)
  matrix products: 88 us -> 0 us
  waiting for transfers between devices: 83.1 us -> 0 us
  blocking collectives: 49.9 us -> 0 us
  Pallas kernels: 0 us -> 36.9 us
  between operations: 21.7 us -> 1.86 us
  other arithmetic: 19.7 us -> 2.62 us
  starting transfers between devices: 7.36 us -> 0 us
    dot_general x4 -> x0, matrix products: 88 us -> none  [fisher_block(): grad = jnp.dot(left.T, right, preferred_element_type=jnp.float32)]
    reduce_scatter x2 -> x0, waiting for transfers between devices: 82.4 us -> none  [the longest x1 43.7 us: shards(): lax.psum_scatter(fisher, 'mp', scatter_dimension=1, tiled=True)]
    all_gather x2 -> x0, blocking collectives: 49.9 us -> none  [the longest x1 38.1 us: shards(): lax.all_gather(grads, 'dp', axis=0, tiled=True)]
    pallas_call x0 -> x1, Pallas kernels: none -> 36.9 us  [shards_kernel(): pl.pallas_call(functools.partial(merge_kernel, sources), out_shape=pltpu....]
    div x1 -> x0, other arithmetic: 15.7 us -> none  [shards(): return num_half / (den_half + fisher_eps)]
    all_to_all x1 -> x0, starting transfers between devices: 7.28 us -> none  [shards(): lax.all_to_all(acts, 'dp', split_axis=1, concat_axis=0, tiled=True)]
  transfers between devices with their start and end apart: 3 -> 0, of which waited for: 2 -> 0; matrix products, arithmetic and copies ran while one was open for 4% -> 0% of each run, Pallas kernels for 0% -> 0%
where the time goes in v2:
time: 50.3 us; the launch traced here: 50 us
  Pallas kernels  36.9 us (73%)
  local copies, waits for them, and re-layouts  8.59 us (17%)
  other arithmetic  2.62 us (5%)
  between operations  1.86 us (4%)
    pallas_call x1, Pallas kernels, shards_kernel(): pl.pallas_call(functools.partial(merge_kernel, sources), out_shape=pltpu....  36.9 us
    unnamed x1, local copies, waits for them, and re-layouts  5.47 us
    reshape x1, local copies, waits for them, and re-layouts, shards_kernel(): g_pack = g_pack.reshape(MODELS, chunks, packed, WIDE)  1.57 us
    concatenate x1, other arithmetic, shards_kernel(): x_pack = jnp.concatenate([x_part, code], axis=2)  1.39 us
    slice x1, local copies, waits for them, and re-layouts, shards_kernel(): end = end + lens[e]  1.38 us
    add x1, other arithmetic, shards_kernel(): (lax.axis_index('mp') * EXAMPLES + example)[None, :] * QUARTERS  1.22 us

profile of v2, /device:TPU:0, one launch (start us, length us, event | category | flops | bytes accessed | tf_op | source)
XLA Modules:
  0.0 50.0 jit_solution(18029466762466574002)
XLA Ops:
  0.0 1.4 %fusion.5 = (s32[1,1]{1,0:T(1,128)}, s32[1,1]{1,0:T(1,128)}, s32[1,1]{1,0:T(1,128)}) fusion(s32[1,4]{1,0:T(1,128)} %param.8), kind=kLoop, calls=%fused_computation.10 | loop fusion | bytes 24 | tf_op jit(solution)/shard_map/slice | solution.py:208
  3.2 1.2 %fusion.4 = s32[4]{0:T(128)S(1)} fusion(s32[1,4]{1,0:T(1,128)} %param.7, s32[]{:T(128)S(6)} %add.44, s32[]{:T(128)S(6)} %add.42, s32[]{:T(128)} %bitcast.3, s32[]{:T(128)S(6)} %mul.8), kind=kLoop, calls=%fused_computation.9 | loop fusion | flops 40 | bytes 48 | tf_op jit(solution)/shard_map/add | solution.py:210
  4.5 0.1 convert_element_type.23
  4.5 0.1 broadcast_in_dim.2
  4.6 1.4 %pad_maximum_fusion.x_ref = bf16[8,16,256]{2,1,0:T(8,128)(2,1)} fusion(bf16[8,16,128]{2,1,0:T(8,128)(2,1)S(1)} %broadcast_in_dim.2, bf16[8,16,128]{2,1,0:T(8,128)(2,1)} %bitcast.15), kind=kLoop, calls=%fused_computation | loop fusion | flops 131072 | bytes 131072 | tf_op jit(solution)/shard_map/concatenate | solution.py:213
  6.0 1.6 %reshape.30.g_ref = bf16[2,7,16,256]{3,2,1,0:T(8,128)(2,1)} reshape(bf16[2,7,4,4,256]{4,3,2,1,0:T(4,128)(2,1)} %bitcast.14) | data formatting | bytes 229376 | tf_op jit(solution)/shard_map/reshape | solution.py:215
  7.6 36.9 %merge.1 = f32[512,7168]{1,0:T(8,128)S(1)} custom-call(bf16[8,16,256]{2,1,0:T(8,128)(2,1)} %pad_maximum_fusion.x_ref, bf16[2,7,16,256]{3,2,1,0:T(8,128)(2,1)} %reshape.30.g_ref, bf16[512,14336]{1,0:T(8,128)(2,1)} %bitcast.16), custom_call_target="tpu_custom_call" | custom-call | flops 15032385536 | bytes 44040192 | tf_op jit(solution)/shard_map/merge/pallas_call | solution.py:218
  44.5 5.5 %copy.9 = f32[512,7168]{1,0:T(8,128)} copy(f32[512,7168]{1,0:T(8,128)S(1)} %merge.1) | data formatting | bytes 29360128
  (1 shorter events, 0.0 us)

commit v3 on v2

--- a/solution.py
+++ b/solution.py
@@ -67,7 +67,7 @@
     return num_half / (den_half + fisher_eps)
 
 
-def merge_kernel(sources, x_ref, g_ref, w_ref, out_ref, x_all, g_all, lhs, w_own, w_mate,
+def merge_kernel(sources, slots_ref, lens_ref, acts_ref, grads_ref, w_ref, out_ref, x_ref, g_ref, x_all, g_all, lhs, w_own, w_mate,
                  x_recv, line_recv, relay_recv, w_recv, own_sem, x_send, line_send, relay_send, w_send):
     mp, dp = lax.axis_index("mp"), lax.axis_index("dp")
     mate = 1 - mp
@@ -114,6 +114,30 @@
     for to_mp, to_dp in places:
         pl.semaphore_signal(barrier, inc=1, device_id={"mp": to_mp, "dp": to_dp},
                             device_id_type=pl.DeviceIdType.MESH)
+
+    tokens = acts_ref.shape[0]
+    packed = QUARTERS * tokens
+    row = lax.broadcasted_iota(jnp.int32, (packed, LANES), 0)
+    code = row // tokens
+    for i in range(tokens):
+        end, example = 0, 0
+        for e in range(EXAMPLES - 1):
+            end = end + lens_ref[0, e]
+            example = example + jnp.where(slots_ref[0, i] >= end, 1, 0)
+        code = code + jnp.where(row % tokens == i, (mp * EXAMPLES + example) * QUARTERS, 0)
+    code = code.astype(jnp.float32).astype(jnp.bfloat16)
+
+    def stacked(ref, start, width):
+        parts = [ref[:, start + q * width:start + (q + 1) * width].astype(jnp.float32) for q in range(QUARTERS)]
+        return jnp.concatenate(parts, axis=0).astype(jnp.bfloat16)
+
+    for m in range(MODELS):
+        for c in range(chunks):
+            g_ref[m, c] = stacked(grads_ref, m * cols + c * step, WIDE)
+    for k in range(sources):
+        x_ref[k, :, :LANES] = stacked(acts_ref, k * rows, LANES)
+        x_ref[k, :, LANES:] = code
+
     pltpu.make_async_copy(x_ref.at[dp], x_all.at[line, spot, mp], x_recv).start()
 
     @pl.loop(0, chunks)
@@ -139,10 +163,8 @@
 
     pltpu.make_async_copy(x_all, x_all, x_recv).wait()
     arrived = x_all[...].reshape(DEPTH, 2 * LANES).astype(jnp.float32).T
-    code = arrived[LANES:LANES + 1, :]
+    marks = arrived[LANES:LANES + 1, :]
     arrived = arrived[:LANES, :].astype(jnp.bfloat16)
-    tokens = DEPTH // (MODELS * sources * QUARTERS)
-    packed = QUARTERS * tokens
     source = lax.broadcasted_iota(jnp.int32, (DEPTH, DEPTH), 0)
     target = lax.broadcasted_iota(jnp.int32, (DEPTH, DEPTH), 1)
     same = (source // packed == target // packed) & (source % tokens == target % tokens)
@@ -153,15 +175,11 @@
         for q in range(QUARTERS):
             for v in range(STACK):
                 which = lax.rem(mp + v // EXAMPLES, MODELS) * EXAMPLES + v % EXAMPLES
-                keep = code == (which * QUARTERS + q).astype(jnp.float32)
+                keep = marks == (which * QUARTERS + q).astype(jnp.float32)
                 lhs[q, t, v * SUB + base:v * SUB + base + LANES, :] = left * keep.astype(jnp.float32).astype(jnp.bfloat16)
 
     @pl.loop(0, chunks)
     def _(c):
-        @pl.when(c + 2 < chunks)
-        def _():
-            relay(c + 2)
-
         other_line = g_all.at[c, 1 - line]
         pltpu.make_async_copy(other_line, other_line, relay_recv.at[c]).wait()
         own_copy(c).wait()
@@ -169,6 +187,10 @@
 
         @pl.loop(0, rows // SUB)
         def _(t):
+            @pl.when((t == rows // SUB - 1) & (c + 2 < chunks))
+            def _():
+                relay(c + 2)
+
             at = pl.ds(pl.multiple_of(t * SUB, SUB), SUB)
             for q in range(QUARTERS):
                 right = g_all[c].reshape(DEPTH, WIDE)
@@ -196,31 +218,27 @@
 
 
 def shards_kernel(activations, out_grads, slot_of, lengths, weights):
-    acts, grads, slots, lens, w_shard = activations[0], out_grads[0], slot_of[0], lengths[0], weights[0]
+    acts, grads, w_shard = activations[0], out_grads[0], weights[0]
     sources = lax.axis_size("dp")
     tokens, width = acts.shape
     rows = width // sources
     cols = grads.shape[1] // MODELS
     chunks = cols // (QUARTERS * WIDE)
     packed = QUARTERS * tokens
-    example, end = jnp.zeros((tokens,), jnp.int32), 0
-    for e in range(EXAMPLES - 1):
-        end = end + lens[e]
-        example = example + (slots >= end).astype(jnp.int32)
-    code = (lax.axis_index("mp") * EXAMPLES + example)[None, :] * QUARTERS + jnp.arange(QUARTERS)[:, None]
-    x_part = acts.reshape(tokens, sources, rows // LANES, LANES).transpose(1, 2, 0, 3).reshape(sources, packed, LANES)
-    code = jnp.broadcast_to(code.reshape(1, packed, 1), (sources, packed, LANES)).astype(jnp.bfloat16)
-    x_pack = jnp.concatenate([x_part, code], axis=2)
-    g_pack = grads.reshape(tokens, MODELS, chunks, QUARTERS, WIDE).transpose(1, 2, 3, 0, 4)
-    g_pack = g_pack.reshape(MODELS, chunks, packed, WIDE)
     length = sources // LINES
     dma = pltpu.SemaphoreType.DMA
     return pl.pallas_call(
         functools.partial(merge_kernel, sources),
         out_shape=pltpu.VMEM((rows, cols), jnp.float32),
-        in_specs=[pl.BlockSpec(memory_space=pl.ANY)] * 3,
+        in_specs=[
+            pl.BlockSpec(memory_space=pltpu.SMEM), pl.BlockSpec(memory_space=pltpu.SMEM),
+            pl.BlockSpec(memory_space=pltpu.VMEM), pl.BlockSpec(memory_space=pltpu.VMEM),
+            pl.BlockSpec(memory_space=pl.ANY),
+        ],
         out_specs=pl.BlockSpec(memory_space=pltpu.VMEM),
         scratch_shapes=[
+            pltpu.VMEM((sources, packed, 2 * LANES), jnp.bfloat16),
+            pltpu.VMEM((MODELS, chunks, packed, WIDE), jnp.bfloat16),
             pltpu.VMEM((LINES, length, MODELS, packed, 2 * LANES), jnp.bfloat16),
             pltpu.VMEM((chunks, LINES, length, MODELS, packed, WIDE), jnp.bfloat16),
             pltpu.VMEM((QUARTERS, rows // SUB, STACK * SUB, DEPTH), jnp.bfloat16),
@@ -234,7 +252,7 @@
         cost_estimate=pl.CostEstimate(
             flops=2 * STACK * rows * cols * DEPTH, bytes_accessed=12 * rows * cols, transcendentals=0),
         name="merge",
-    )(x_pack, g_pack, w_shard)
+    )(slot_of, lengths, acts, grads, w_shard)
 
 
 def solution(mesh):

time: 50.3 us -> 42.8 us (0.85)
  local copies, waits for them, and re-layouts: 8.59 us -> 5.47 us
  other arithmetic: 2.62 us -> 0 us
  between operations: 1.86 us -> 0.01 us
    reshape x1 -> x0, local copies, waits for them, and re-layouts: 1.57 us -> none  [shards_kernel(): g_pack = g_pack.reshape(MODELS, chunks, packed, WIDE)]
    concatenate x1 -> x0, other arithmetic: 1.39 us -> none  [shards_kernel(): x_pack = jnp.concatenate([x_part, code], axis=2)]
    slice x1 -> x0, local copies, waits for them, and re-layouts: 1.38 us -> none  [shards_kernel(): end = end + lens[e]]
    add x1 -> x0, other arithmetic: 1.22 us -> none  [shards_kernel(): (lax.axis_index('mp') * EXAMPLES + example)[None, :] * QUARTERS]
where the time goes in v3:
time: 42.8 us; the launch traced here: 42.7 us
  Pallas kernels  37.2 us (87%)
  local copies, waits for them, and re-layouts  5.47 us (13%)
    pallas_call x1, Pallas kernels, shards_kernel(): pl.pallas_call(functools.partial(merge_kernel, sources), out_shape=pltpu....  37.2 us
    unnamed x1, local copies, waits for them, and re-layouts  5.47 us

profile of v3, /device:TPU:0, one launch (start us, length us, event | category | flops | bytes accessed | tf_op | source)
XLA Modules:
  0.0 42.7 jit_solution(7942575374817170035)
XLA Ops:
  0.0 37.2 %merge.1 = f32[512,7168]{1,0:T(8,128)S(1)} custom-call(s32[1,4]{1,0:T(1,128)} %slots_ref.1, s32[1,4]{1,0:T(1,128)} %lens_ref.1, bf16[4,4096]{1,0:T(4,128)(2,1)} %bitcast.5, bf16[4,14336]{1,0:T(4,128)(2,1)} %bitcast.4, bf16[512,14336]{1,0:T(8,128)(2,1)} %bitcast.3), custom_call_target="tpu_custom_call" | custom-call | flops 15032385536 | bytes 44040192 | tf_op jit(solution)/shard_map/merge/pallas_call | solution.py:230
  37.2 5.5 %copy.7 = f32[512,7168]{1,0:T(8,128)} copy(f32[512,7168]{1,0:T(8,128)S(1)} %merge.1) | data formatting | bytes 29360128

commit v4 on v3

--- a/solution.py
+++ b/solution.py
@@ -67,14 +67,62 @@
     return num_half / (den_half + fisher_eps)
 
 
-def merge_kernel(sources, slots_ref, lens_ref, acts_ref, grads_ref, w_ref, out_ref, x_ref, g_ref, x_all, g_all, lhs, w_own, w_mate,
+def chunk_rows(c, t, lhs, g_all, w_own, w_mate, store):
+    at = pl.ds(pl.multiple_of(t * SUB, SUB), SUB)
+    for q in range(QUARTERS):
+        right = g_all[c].reshape(DEPTH, WIDE)
+        fishers = []
+        for h in range(MODELS):
+            fisher = jnp.zeros((SUB, WIDE), jnp.float32)
+            for e in range(EXAMPLES):
+                v = h * EXAMPLES + e
+                grad = jnp.dot(lhs[q, t, v * SUB:(v + 1) * SUB, :], right, preferred_element_type=jnp.float32)
+                fisher = fisher + grad * grad
+            fishers.append(fisher)
+        own, other = fishers
+        here = pl.ds(pl.multiple_of((c * QUARTERS + q) * WIDE, WIDE), WIDE)
+        top = own * w_own[at, here].astype(jnp.float32) + other * w_mate[at, here].astype(jnp.float32)
+        store(at, here, top / (own + other + fisher_eps))
+
+
+def finish_kernel(early_ref, lhs, g_all, w_own, w_mate, out_ref, late, sem):
+    rows, done = early_ref.shape
+    step = QUARTERS * WIDE
+    chunks, first = out_ref.shape[1] // step, done // step
+    write = pltpu.make_async_copy(early_ref, out_ref.at[:, pl.ds(0, done)], sem.at[chunks - first])
+    write.start()
+
+    def out_copy(c):
+        return pltpu.make_async_copy(
+            late.at[:, pl.ds(pl.multiple_of((c - first) * step, LANES), step)],
+            out_ref.at[:, pl.ds(pl.multiple_of(c * step, LANES), step)], sem.at[c - first])
+
+    @pl.loop(first, chunks)
+    def _(c):
+        @pl.loop(0, rows // SUB)
+        def _(t):
+            def store(at, here, value):
+                late[at, pl.ds(pl.multiple_of(here.start - done, WIDE), WIDE)] = value
+
+            chunk_rows(c, t, lhs, g_all, w_own, w_mate, store)
+
+        out_copy(c).start()
+
+    @pl.loop(first, chunks)
+    def _(c):
+        out_copy(c).wait()
+
+    write.wait()
+
+
+def merge_kernel(sources, slots_ref, lens_ref, acts_ref, grads_ref, w_ref, early_ref, lhs, g_all, w_own, w_mate, x_ref, g_ref, x_all,
                  x_recv, line_recv, relay_recv, w_recv, own_sem, x_send, line_send, relay_send, w_send):
     mp, dp = lax.axis_index("mp"), lax.axis_index("dp")
     mate = 1 - mp
     line, spot = lax.rem(dp, LINES), lax.div(dp, LINES)
     length = sources // LINES
-    rows, cols = out_ref.shape
-    chunks = g_ref.shape[1]
+    rows, cols = w_own.shape
+    chunks, early = g_ref.shape[1], early_ref.shape[1] // (QUARTERS * WIDE)
     step = QUARTERS * WIDE
 
     def send(src, dst, send_sem, recv_sem, to_mp, to_dp):
@@ -178,12 +226,15 @@
                 keep = marks == (which * QUARTERS + q).astype(jnp.float32)
                 lhs[q, t, v * SUB + base:v * SUB + base + LANES, :] = left * keep.astype(jnp.float32).astype(jnp.bfloat16)
 
-    @pl.loop(0, chunks)
-    def _(c):
+    def arrive(c):
         other_line = g_all.at[c, 1 - line]
         pltpu.make_async_copy(other_line, other_line, relay_recv.at[c]).wait()
         own_copy(c).wait()
         w_copy(c).wait_recv()
+
+    @pl.loop(0, early)
+    def _(c):
+        arrive(c)
 
         @pl.loop(0, rows // SUB)
         def _(t):
@@ -191,21 +242,12 @@
             def _():
                 relay(c + 2)
 
-            at = pl.ds(pl.multiple_of(t * SUB, SUB), SUB)
-            for q in range(QUARTERS):
-                right = g_all[c].reshape(DEPTH, WIDE)
-                fishers = []
-                for h in range(MODELS):
-                    fisher = jnp.zeros((SUB, WIDE), jnp.float32)
-                    for e in range(EXAMPLES):
-                        v = h * EXAMPLES + e
-                        grad = jnp.dot(lhs[q, t, v * SUB:(v + 1) * SUB, :], right, preferred_element_type=jnp.float32)
-                        fisher = fisher + grad * grad
-                    fishers.append(fisher)
-                own, other = fishers
-                here = pl.ds(pl.multiple_of(c * step + q * WIDE, LANES), WIDE)
-                top = own * w_own[at, here].astype(jnp.float32) + other * w_mate[at, here].astype(jnp.float32)
-                out_ref[at, here] = top / (own + other + fisher_eps)
+            def store(at, here, value):
+                early_ref[at, here] = value
+
+            chunk_rows(c, t, lhs, g_all, w_own, w_mate, store)
+
+    pl.loop(early, chunks)(arrive)
 
     blocks = lambda count: lhs.at[0, 0, pl.ds(0, count * packed)]
     pltpu.make_async_copy(blocks(len(places)), blocks(len(places)), x_send).wait()
@@ -227,32 +269,45 @@
     packed = QUARTERS * tokens
     length = sources // LINES
     dma = pltpu.SemaphoreType.DMA
-    return pl.pallas_call(
+    early = chunks - 2
+    kept = [
+        ((rows, early * QUARTERS * WIDE), jnp.float32),
+        ((QUARTERS, rows // SUB, STACK * SUB, DEPTH), jnp.bfloat16),
+        ((chunks, LINES, length, MODELS, packed, WIDE), jnp.bfloat16),
+        ((rows, cols), jnp.bfloat16),
+        ((rows, cols), jnp.bfloat16),
+    ]
+    vmem, anywhere = pl.BlockSpec(memory_space=pltpu.VMEM), pl.BlockSpec(memory_space=pl.ANY)
+    smem = pl.BlockSpec(memory_space=pltpu.SMEM)
+    handed = pl.pallas_call(
         functools.partial(merge_kernel, sources),
-        out_shape=pltpu.VMEM((rows, cols), jnp.float32),
-        in_specs=[
-            pl.BlockSpec(memory_space=pltpu.SMEM), pl.BlockSpec(memory_space=pltpu.SMEM),
-            pl.BlockSpec(memory_space=pltpu.VMEM), pl.BlockSpec(memory_space=pltpu.VMEM),
-            pl.BlockSpec(memory_space=pl.ANY),
-        ],
-        out_specs=pl.BlockSpec(memory_space=pltpu.VMEM),
+        out_shape=[pltpu.VMEM(*one) for one in kept],
+        in_specs=[smem, smem, vmem, vmem, anywhere],
+        out_specs=[vmem] * len(kept),
         scratch_shapes=[
             pltpu.VMEM((sources, packed, 2 * LANES), jnp.bfloat16),
             pltpu.VMEM((MODELS, chunks, packed, WIDE), jnp.bfloat16),
             pltpu.VMEM((LINES, length, MODELS, packed, 2 * LANES), jnp.bfloat16),
-            pltpu.VMEM((chunks, LINES, length, MODELS, packed, WIDE), jnp.bfloat16),
-            pltpu.VMEM((QUARTERS, rows // SUB, STACK * SUB, DEPTH), jnp.bfloat16),
-            pltpu.VMEM((rows, cols), jnp.bfloat16),
-            pltpu.VMEM((rows, cols), jnp.bfloat16),
             dma, dma((chunks,)), dma((chunks,)), dma((chunks,)), dma((chunks,)),
             dma, dma((chunks,)), dma((chunks,)), dma((chunks,)),
         ],
         compiler_params=pltpu.CompilerParams(
-            collective_id=0, has_side_effects=True, vmem_limit_bytes=40 * 1024 * 1024),
-        cost_estimate=pl.CostEstimate(
-            flops=2 * STACK * rows * cols * DEPTH, bytes_accessed=12 * rows * cols, transcendentals=0),
+            collective_id=0, has_side_effects=True, vmem_limit_bytes=12 * 1024 * 1024),
         name="merge",
     )(slot_of, lengths, acts, grads, w_shard)
+    handed = [pltpu.with_memory_space_constraint(one, pltpu.VMEM) for one in handed]
+    return pl.pallas_call(
+        finish_kernel,
+        out_shape=jax.ShapeDtypeStruct((rows, cols), jnp.float32),
+        in_specs=[vmem] * len(kept),
+        out_specs=anywhere,
+        scratch_shapes=[
+            pltpu.VMEM((rows, (chunks - early) * QUARTERS * WIDE), jnp.float32),
+            dma((chunks - early + 1,)),
+        ],
+        compiler_params=pltpu.CompilerParams(vmem_limit_bytes=12 * 1024 * 1024),
+        name="finish",
+    )(*handed)
 
 
 def solution(mesh):

time: 42.8 us -> 44.9 us (1.049)
  Pallas kernels: 37.2 us -> 41.7 us
  local copies, waits for them, and re-layouts: 5.47 us -> 2.96 us
    pallas_call x1 -> x2, Pallas kernels: 37.2 us -> 41.7 us  [the longest x1 34.4 us: shards_kernel(): pl.pallas_call(functools.partial(merge_kernel, sources), out_shape=[pltpu...]
    unnamed x1 -> x8, local copies, waits for them, and re-layouts: 5.47 us -> 2.96 us
where the time goes in v4:
time: 44.9 us; the launch traced here: 44.7 us
  Pallas kernels  41.7 us (93%)
  local copies, waits for them, and re-layouts  2.96 us (7%)
    pallas_call x1, Pallas kernels, shards_kernel(): pl.pallas_call(functools.partial(merge_kernel, sources), out_shape=[pltpu...  34.4 us
    pallas_call x1, Pallas kernels, shards_kernel(): pl.pallas_call(finish_kernel, out_shape=jax.ShapeDtypeStruct((rows, cols)...  7.28 us
    unnamed x8, local copies, waits for them, and re-layouts  2.96 us

profile of v4, /device:TPU:0, one launch (start us, length us, event | category | flops | bytes accessed | tf_op | source)
XLA Modules:
  0.0 44.7 jit_solution(17697677249484528572)
XLA Ops:
  0.0 0.0 copy-start
  0.0 0.9 %copy-done = bf16[1,4,14336]{2,1,0:T(4,128)(2,1)S(1)} copy-done((bf16[1,4,14336]{2,1,0:T(4,128)(2,1)S(1)}, bf16[1,4,14336]{2,1,0:T(4,128)(2,1)}, u32[]{:S(2)}) %copy-start) | copy-done | bytes 114712
  0.9 0.0 copy-start.1
  0.9 0.8 %copy-done.1 = bf16[1,4,4096]{2,1,0:T(4,128)(2,1)S(1)} copy-done((bf16[1,4,4096]{2,1,0:T(4,128)(2,1)S(1)}, bf16[1,4,4096]{2,1,0:T(4,128)(2,1)}, u32[]{:S(2)}) %copy-start.1) | copy-done | bytes 32792
  1.7 0.0 copy-start.2
  1.7 0.7 %copy-done.2 = s32[1,4]{1,0:T(1,128)S(1)} copy-done((s32[1,4]{1,0:T(1,128)S(1)}, s32[1,4]{1,0:T(1,128)}, u32[]{:S(2)}) %copy-start.2) | copy-done | bytes 40
  2.3 0.0 copy-start.3
  2.3 0.7 %copy-done.3 = s32[1,4]{1,0:T(1,128)S(1)} copy-done((s32[1,4]{1,0:T(1,128)S(1)}, s32[1,4]{1,0:T(1,128)}, u32[]{:S(2)}) %copy-start.3) | copy-done | bytes 40
  3.0 34.4 %merge.1 = (f32[512,5120]{1,0:T(8,128)S(1)}, bf16[4,2,2048,256]{3,2,1,0:T(8,128)(2,1)S(1)}, bf16[7,2,4,2,16,256]{5,4,3,2,1,0:T(8,128)(2,1)S(1)}, bf16[512,7168]{1,0:T(8,128)(2,1)S(1)}, bf16[512,7168]{1,0:T(8,128)(2,1)S(1)}) custom-call(s32[1,4]{1,0:T(1,128)S(1)} %copy-done.2, s32[1,4]{1,0:T(1,128)S(1)} %copy-done.3, bf16[4,4096]{1,0:T(4,128)(2,1)S(1)} %bitcast.4, ...), custom_call_target="tpu_custom_call" | custom-call | tf_op jit(solution)/shard_map/merge/pallas_call | solution.py:282
  37.4 7.3 %finish.1 = f32[512,7168]{1,0:T(8,128)} custom-call(f32[512,5120]{1,0:T(8,128)S(1)} %get-tuple-element.10.early_ref, bf16[4,2,2048,256]{3,2,1,0:T(8,128)(2,1)S(1)} %get-tuple-element.11.lhs, bf16[7,2,4,2,16,256]{5,4,3,2,1,0:T(8,128)(2,1)S(1)} %get-tuple-element.12.g_all, bf16[512,7168]{1,0:T(8,128)(2,1)S(1)} %get-tuple-element.13.w_own, ...), custom_call_target="tpu_custom_call" | custom-call | tf_op jit(solution)/shard_map/finish/pallas_call | solution.py:299
Async XLA Ops:
  0.0 0.9 %copy-start = (bf16[1,4,14336]{2,1,0:T(4,128)(2,1)S(1)}, bf16[1,4,14336]{2,1,0:T(4,128)(2,1)}, u32[]{:S(2)}) copy-start(bf16[1,4,14336]{2,1,0:T(4,128)(2,1)} %param.6) | copy-start | bytes 344068
  0.9 0.8 %copy-start.1 = (bf16[1,4,4096]{2,1,0:T(4,128)(2,1)S(1)}, bf16[1,4,4096]{2,1,0:T(4,128)(2,1)}, u32[]{:S(2)}) copy-start(bf16[1,4,4096]{2,1,0:T(4,128)(2,1)} %param.5) | copy-start | bytes 98308
  1.7 0.7 %copy-start.2 = (s32[1,4]{1,0:T(1,128)S(1)}, s32[1,4]{1,0:T(1,128)}, u32[]{:S(2)}) copy-start(s32[1,4]{1,0:T(1,128)} %slots_ref.1) | copy-start | bytes 52
  2.3 0.7 %copy-start.3 = (s32[1,4]{1,0:T(1,128)S(1)}, s32[1,4]{1,0:T(1,128)}, u32[]{:S(2)}) copy-start(s32[1,4]{1,0:T(1,128)} %lens_ref.1) | copy-start | bytes 52

commit v5 on v4

--- a/solution.py
+++ b/solution.py
@@ -238,9 +238,15 @@
 
         @pl.loop(0, rows // SUB)
         def _(t):
-            @pl.when((t == rows // SUB - 1) & (c + 2 < chunks))
+            part = c * (rows // SUB) + t
+
+            @pl.when(part == 1)
             def _():
-                relay(c + 2)
+                relay(2)
+
+            @pl.when((part >= 3) & (part < chunks))
+            def _():
+                relay(part)
 
             def store(at, here, value):
                 early_ref[at, here] = value
@@ -294,7 +300,7 @@
         compiler_params=pltpu.CompilerParams(
             collective_id=0, has_side_effects=True, vmem_limit_bytes=12 * 1024 * 1024),
         name="merge",
-    )(slot_of, lengths, acts, grads, w_shard)
+    )(*[pltpu.with_memory_space_constraint(one, pltpu.HBM) for one in (slot_of, lengths, acts, grads)], w_shard)
     handed = [pltpu.with_memory_space_constraint(one, pltpu.VMEM) for one in handed]
     return pl.pallas_call(
         finish_kernel,

time: 44.9 us -> 39.1 us (0.87)
  local copies, waits for them, and re-layouts: 2.96 us -> 0 us
  Pallas kernels: 41.7 us -> 39 us
    unnamed x8 -> x0, local copies, waits for them, and re-layouts: 2.96 us -> none
    pallas_call x1, Pallas kernels: 34.4 us -> 32.1 us  [shards_kernel(): pl.pallas_call(functools.partial(merge_kernel, sources), out_shape=[pltpu...]
where the time goes in v5:
time: 39.1 us; the launch traced here: 39 us
  Pallas kernels  39 us (100%)
    pallas_call x1, Pallas kernels, shards_kernel(): pl.pallas_call(functools.partial(merge_kernel, sources), out_shape=[pltpu...  32.1 us
    pallas_call x1, Pallas kernels, shards_kernel(): pl.pallas_call(finish_kernel, out_shape=jax.ShapeDtypeStruct((rows, cols)...  6.88 us

profile of v5, /device:TPU:0, one launch (start us, length us, event | category | flops | bytes accessed | tf_op | source)
XLA Modules:
  0.0 39.0 jit_solution(11323016835875026952)
XLA Ops:
  0.0 32.1 %merge.1 = (f32[512,5120]{1,0:T(8,128)S(1)}, bf16[4,2,2048,256]{3,2,1,0:T(8,128)(2,1)S(1)}, bf16[7,2,4,2,16,256]{5,4,3,2,1,0:T(8,128)(2,1)S(1)}, bf16[512,7168]{1,0:T(8,128)(2,1)S(1)}, bf16[512,7168]{1,0:T(8,128)(2,1)S(1)}) custom-call(s32[1,4]{1,0:T(1,128)} %slots_ref.1, s32[1,4]{1,0:T(1,128)} %lens_ref.1, bf16[4,4096]{1,0:T(4,128)(2,1)} %bitcast.5, ...), custom_call_target="tpu_custom_call" | custom-call | tf_op jit(solution)/shard_map/merge/pallas_call | solution.py:288
  32.1 6.9 %finish.1 = f32[512,7168]{1,0:T(8,128)} custom-call(f32[512,5120]{1,0:T(8,128)S(1)} %get-tuple-element.10.early_ref, bf16[4,2,2048,256]{3,2,1,0:T(8,128)(2,1)S(1)} %get-tuple-element.11.lhs, bf16[7,2,4,2,16,256]{5,4,3,2,1,0:T(8,128)(2,1)S(1)} %get-tuple-element.12.g_all, bf16[512,7168]{1,0:T(8,128)(2,1)S(1)} %get-tuple-element.13.w_own, ...), custom_call_target="tpu_custom_call" | custom-call | tf_op jit(solution)/shard_map/finish/pallas_call | solution.py:305

commit v6 on v5

--- a/solution.py
+++ b/solution.py
@@ -207,7 +207,6 @@
         w_copy(c).start()
 
     relay(0)
-    relay(1)
 
     pltpu.make_async_copy(x_all, x_all, x_recv).wait()
     arrived = x_all[...].reshape(DEPTH, 2 * LANES).astype(jnp.float32).T
@@ -225,6 +224,8 @@
                 which = lax.rem(mp + v // EXAMPLES, MODELS) * EXAMPLES + v % EXAMPLES
                 keep = marks == (which * QUARTERS + q).astype(jnp.float32)
                 lhs[q, t, v * SUB + base:v * SUB + base + LANES, :] = left * keep.astype(jnp.float32).astype(jnp.bfloat16)
+
+    relay(1)
 
     def arrive(c):
         other_line = g_all.at[c, 1 - line]

time: 39.1 us -> 38.5 us (0.985)
  Pallas kernels: 39 us -> 38.4 us
    pallas_call x1, Pallas kernels: 32.1 us -> 31.5 us  [shards_kernel(): pl.pallas_call(functools.partial(merge_kernel, sources), out_shape=[pltpu...]
where the time goes in v6:
time: 38.5 us; the launch traced here: 38.4 us
  Pallas kernels  38.4 us (100%)
    pallas_call x1, Pallas kernels, shards_kernel(): pl.pallas_call(functools.partial(merge_kernel, sources), out_shape=[pltpu...  31.5 us
    pallas_call x1, Pallas kernels, shards_kernel(): pl.pallas_call(finish_kernel, out_shape=jax.ShapeDtypeStruct((rows, cols)...  6.88 us

profile of v6, /device:TPU:0, one launch (start us, length us, event | category | flops | bytes accessed | tf_op | source)
XLA Modules:
  0.0 38.4 jit_solution(14682157509816240849)
XLA Ops:
  0.0 31.5 %merge.1 = (f32[512,5120]{1,0:T(8,128)S(1)}, bf16[4,2,2048,256]{3,2,1,0:T(8,128)(2,1)S(1)}, bf16[7,2,4,2,16,256]{5,4,3,2,1,0:T(8,128)(2,1)S(1)}, bf16[512,7168]{1,0:T(8,128)(2,1)S(1)}, bf16[512,7168]{1,0:T(8,128)(2,1)S(1)}) custom-call(s32[1,4]{1,0:T(1,128)} %slots_ref.1, s32[1,4]{1,0:T(1,128)} %lens_ref.1, bf16[4,4096]{1,0:T(4,128)(2,1)} %bitcast.5, ...), custom_call_target="tpu_custom_call" | custom-call | tf_op jit(solution)/shard_map/merge/pallas_call | solution.py:289
  31.5 6.9 %finish.1 = f32[512,7168]{1,0:T(8,128)} custom-call(f32[512,5120]{1,0:T(8,128)S(1)} %get-tuple-element.10.early_ref, bf16[4,2,2048,256]{3,2,1,0:T(8,128)(2,1)S(1)} %get-tuple-element.11.lhs, bf16[7,2,4,2,16,256]{5,4,3,2,1,0:T(8,128)(2,1)S(1)} %get-tuple-element.12.g_all, bf16[512,7168]{1,0:T(8,128)(2,1)S(1)} %get-tuple-element.13.w_own, ...), custom_call_target="tpu_custom_call" | custom-call | tf_op jit(solution)/shard_map/finish/pallas_call | solution.py:306
